TPU v7x, 256 devices: a whole 4x4x8 slice. The times are simulated.
256 devices in a mesh: lat: 8 (over x, y_lo), lon: 32 (over y_hi, z, core).
Axes of the slice: x: 4, y: 4 (y_hi: 2, y_lo: 2; y = y_hi * 2 + y_lo), z: 8, core: 2. Of those that a mesh axis runs over, the one named last changes fastest.
Arguments:
- tokens: bfloat16 [192, 1536, 512], P('lat', 'lon'), may hold values from -6 to 6
- attend_gain: float32 [512], replicated, may hold values from 0.5 to 1.5
- attend_inward: bfloat16 [512, 1536], replicated, may hold values from -0.25 to 0.25
- attend_outward: bfloat16 [512, 512], replicated, may hold values from -0.25 to 0.25
- expand_gain: float32 [512], replicated, may hold values from 0.5 to 1.5
- expand_weight: bfloat16 [512, 2048], replicated, may hold values from -0.25 to 0.25
- reduce_weight: bfloat16 [2048, 512], replicated, may hold values from -0.125 to 0.125
- merge_gain: float32 [2048], replicated, may hold values from 0.5 to 1.5
- merge_weight: bfloat16 [2048, 1024], replicated, may hold values from -0.125 to 0.125
- coarse_gain: float32 [1024], replicated, may hold values from 0.5 to 1.5
- coarse_inward: bfloat16 [1024, 3072], P('lon'), may hold values from -0.1875 to 0.1875
- coarse_outward: bfloat16 [1024, 1024], P('lon'), may hold values from -0.1875 to 0.1875
Outputs:
- coarse_tokens: bfloat16 [96, 768, 1024], P('lat', 'lon')
All inputs are finite; a program needn't handle non-finite values.
Results may differ from a plain program's by a relative error of at most 0.02.
Values may be sent and summed in bfloat16 or wider, within the bound.
A program may use at most 128 MiB of HBM per device.

v0:
```python
import functools

import jax
import jax.numpy as jnp
import numpy as np
from jax import lax
from jax.experimental import pallas as pl
from jax.experimental.pallas import tpu as pltpu
from jax.sharding import PartitionSpec as P

EPS = 1e-05
F32, BF16 = jnp.float32, jnp.bfloat16
MESH = pl.DeviceIdType.MESH
PAD = 80
SCALE = 0.125 * 1.4426950408889634
TAIL = (
    -0.9999952912330627,
    -1.1512510776519775,
    -0.4584643542766571,
    -0.053960103541612625,
    0.008507910184562206,
    -0.0009305300191044807,
    6.159897748148069e-05,
    -1.8348464436712675e-06,
)


ARGS = ("tokens", "g1", "wi", "wo", "g2", "we", "wr", "gm", "wm", "gc", "ci", "co")
TABLES = ("own1", "halo1", "east1", "east2", "join", "leave", "stay", "enter")
BUFFERS = (
    "x", "xe", "c", "fine", "fe", "fc", "s", "z", "w", "qkv", "ctx", "hid", "xw", "qkv1", "ctx1",
    "xn2", "acc",
)
HELD = ("wi", "wo", "we", "wr", "wm", *TABLES)
SEMAPHORES = ("lsem", "hsend", "hrecv", "gsend", "grecv")
NAMES = (*ARGS, *TABLES, "out", *BUFFERS, *("v" + n for n in HELD), *SEMAPHORES)
ORDER = (
    "east1", "own1", "wi", "halo1", "wo", "we", "wr", "east2", "join", "wm",
    "leave", "stay", "enter",
)


def one_hot(rows, cols, pairs):
    table = np.zeros((rows, cols), np.float32)
    for r, c in pairs:
        table[r, c] = 1.0
    return table.astype(jnp.bfloat16)


def window_slot(row, col, across):
    return ((row // 6) * across + col // 12) * PAD + (row % 6) * 12 + col % 12


def tables():
    band = [(r, c) for r in range(6) for c in range(48)]
    own1 = one_hot(
        320, 288, [(window_slot(r, c, 4), r * 48 + c + 6) for r, c in band if c < 42]
    )
    halo1 = np.stack(
        [
            one_hot(
                320,
                64,
                [
                    (window_slot(r, c, 4), (6 * b + 3 + r) * 6 + c - 42 - (32 * b + 16))
                    for r, c in band
                    if c >= 42
                ],
            )
            for b in range(4)
        ]
    )
    east1 = one_hot(48, 384, [(r * 6 + c, r * 48 + c) for r in range(8) for c in range(6)])
    east2 = one_hot(144, 320, [((6 * b + r) * 6 + c, b * PAD + r * 12 + c) for b in range(4) for r in range(6) for c in range(6)])
    grid = [(r, c) for r in range(12) for c in range(24)]
    joins = []
    for a in range(2):
        pairs = []
        for r in range(6):
            for c in range(24):
                for part in range(4):
                    row = 2 * (6 * a + r + 1) + 1 + part % 2
                    col = 2 * (c + 3) + part // 2
                    if col < 48:
                        src = window_slot(row - 12 * a, col, 4)
                    else:
                        src = 960 + row * 6 + col - 48 - (16, 80)[a]
                    pairs.append((part * 160 + window_slot(r, c, 2), src))
        joins.append(one_hot(640, 1056, pairs))
    join = np.stack(joins)
    leave = one_hot(
        160,
        320,
        [((r - 9) * 18 + c, window_slot(r, c, 2)) for r in range(9, 12) for c in range(18)]
        + [(64 + r * 6 + c - 18, window_slot(r, c, 2)) for r in range(9) for c in range(18, 24)]
        + [
            (128 + (r - 9) * 6 + c - 18, window_slot(r, c, 2))
            for r in range(9, 12)
            for c in range(18, 24)
        ],
    )
    stay = one_hot(
        288,
        320,
        [(r * 24 + c, window_slot(r - 3, c - 6, 2)) for r, c in grid if r >= 3 and c >= 6],
    )
    enter = one_hot(
        288,
        160,
        [(r * 24 + c, r * 18 + c - 6) for r, c in grid if r < 3 and c >= 6]
        + [(r * 24 + c, 64 + (r - 3) * 6 + c) for r, c in grid if r >= 3 and c < 6]
        + [(r * 24 + c, 128 + r * 6 + c) for r, c in grid if r < 3 and c < 6],
    )
    return own1, halo1, east1, east2, join, leave, stay, enter


def mm(a, b):
    return jnp.dot(a, b, preferred_element_type=F32)


def norm(v, gain):
    centred = v - jnp.mean(v, axis=-1, keepdims=True)
    variance = jnp.mean(centred * centred, axis=-1, keepdims=True)
    return (centred * lax.rsqrt(variance + EPS) * gain).astype(BF16)


def gelu(x):
    a = jnp.abs(x)
    e = jnp.full_like(x, TAIL[-1])
    for c in TAIL[-2::-1]:
        e = e * a + c
    return jnp.maximum(x, 0.0) - a * jnp.exp2(e)


def key_bias(cut):
    q = lax.broadcasted_iota(jnp.int32, (PAD, PAD), 0)
    k = lax.broadcasted_iota(jnp.int32, (PAD, PAD), 1)
    hidden = k >= 72
    if cut is not None:
        hidden = hidden | (cut & ((q >= 36) != (k >= 36)))
    one = jnp.where(hidden, jnp.float32(-1e30), jnp.float32(0.0))
    return jnp.concatenate([one] * 4, axis=0)


def attend_window(qkv, ctx, row, bias, width):
    lane = lax.broadcasted_iota(jnp.int32, (PAD, 256), 1) // 64
    low = lax.broadcasted_iota(jnp.int32, (PAD, 128), 1) < 64
    rows = pl.ds(row, PAD)
    for quad in range(width // 256):
        at = quad * 256
        q = qkv[rows, at : at + 256]
        k = qkv[rows, width + at : width + at + 256]
        v = qkv[rows, 2 * width + at : 2 * width + at + 256]
        q4 = jnp.concatenate([q * (lane == h).astype(BF16) for h in range(4)], axis=0)
        s = lax.dot_general(q4, k, (((1,), (1,)), ((), ())), preferred_element_type=F32) + bias
        p = jnp.exp2((s - jnp.max(s, axis=-1, keepdims=True)) * SCALE)
        total = jnp.sum(p, axis=-1, keepdims=True)
        o = mm(p.astype(BF16), v) * (1.0 / total)
        left = jnp.where(low, o[0:PAD, 0:128], o[PAD : 2 * PAD, 0:128])
        right = jnp.where(low, o[2 * PAD : 3 * PAD, 128:256], o[3 * PAD :, 128:256])
        ctx[rows, at : at + 128] = left.astype(BF16)
        ctx[rows, at + 128 : at + 256] = right.astype(BF16)


def kernel(remote, *refs):
    r = dict(zip(NAMES, refs, strict=True))
    x, xe, c, fine, fe, fc, s, z, w, qkv, ctx, hid, xw, qkv1, ctx1, xn2, acc = (
        r[n] for n in BUFFERS
    )

    lat, lon = lax.axis_index("lat"), lax.axis_index("lon")
    lats, lons = lax.axis_size("lat"), lax.axis_size("lon")
    zs = max(lons // 4, 1)
    y_lo, core = lat % 2, lon % 2
    zi, y_hi = (lon // 2) % zs, lon // (2 * zs)
    north, south = (lat + lats - 1) % lats, (lat + 1) % lats
    west, east = (lon + lons - 1) % lons, (lon + 1) % lons

    def at_z(k):
        return y_hi * (2 * zs) + ((zi + k + zs) % zs) * 2 + core

    other = (lat - y_lo + (1 - y_lo), (1 - y_hi) * (2 * zs) + zi * 2 + core)
    next_x, last_x = ((lat + 2) % lats, lon), ((lat + lats - 2) % lats, lon)
    twin = (lat, lon - core + (1 - core))
    up_z, down_z = (lat, at_z(1)), (lat, at_z(-1))

    def load(i, src, dst):
        copy = pltpu.make_async_copy(src, dst, r["lsem"].at[i])
        copy.start()
        return copy

    shard = pl.ds(pl.multiple_of(lon * 32, 32), 32)
    load_x = load(0, r["tokens"], x.at[pl.ds(0, 1152)])
    load_ci = load(1, r["ci"], w.at[shard, pl.ds(0, 3072)])
    load_co = load(2, r["co"], w.at[shard, pl.ds(3072, 1024)])
    loads = {}

    def fetch(*which):
        for n in which:
            loads[n] = load(3 + ORDER.index(n), r[n], r["v" + n])

    fetch("east1", "own1", "wi")

    def need(*which):
        for n in which:
            loads.pop(n).wait()

    if remote:
        barrier = pltpu.get_barrier_semaphore()
        partners = [
            (north, lon), (south, lon), (lat, west), (lat, east), (north, west), (south, east),
            up_z, down_z, other, next_x, last_x, twin,
        ]
        for partner in partners:
            pl.semaphore_signal(barrier, inc=1, device_id=partner, device_id_type=MESH)

    def send(pair, i, src, dst, device):
        copy = pltpu.make_async_remote_copy(
            src_ref=src, dst_ref=dst, send_sem=r[pair + "send"].at[i],
            recv_sem=r[pair + "recv"].at[i], device_id=device, device_id_type=MESH,
        )
        if remote:
            copy.start()
        return copy

    sent = []

    def halo(i, src, dst, device):
        copy = send("h", i, src, dst, device)
        sent.append(copy)
        return copy

    def arrive(*copies):
        if remote:
            for copy in copies:
                copy.wait_recv()

    seq = [0, -1, 1, -2, 2, -3, 3, 4]
    pick = (lat // 2) % 2

    def rows_of(half, k, start=0, count=32):
        first = (half * (2 * zs) + ((zi + k + zs) % zs) * 2 + core) * 32 + start
        return w.at[pl.ds(pl.multiple_of(first, 16), count)]

    got = {}

    def push(key, i, ref, device):
        got[key] = send("g", i, ref, ref, device)
        sent.append(got[key])

    def half(k, part):
        return rows_of(y_hi, k, 16 * ((pick + part) % 2), 16)

    def push_up(step, part):
        push(("up", step, part), 2 * step + part, half(-step, part), up_z)

    def push_down(step, part):
        i = 7 + (6 if step == 3 else 2 * step + part)
        push(("down", step, part), i, half(step, part), down_z)

    def push_other(n):
        push(("other", n), 14 + n, half(seq[n], 0), other)

    def push_x(n):
        arrive(got["other", n])
        mine = rows_of(1 - y_hi, seq[n], 16 * pick, 16)
        push(("left", n), 22 + 2 * n, mine.at[:, pl.ds(0, 2048)], last_x)
        push(("right", n), 23 + 2 * n, mine.at[:, pl.ds(2048, 2048)], next_x)

    def push_near(n):
        push(("near", n), 38 + n, rows_of(y_hi, seq[n]), twin)

    def push_far(n):
        arrive(got["left", n], got["right", n])
        push(("far", n), 46 + n, rows_of(1 - y_hi, seq[n]), twin)

    def gather_round(j):
        if j == 0:
            load_ci.wait()
            load_co.wait()
            for part in range(2):
                push_up(0, part)
                push_down(0, part)
            push_other(0)
            push_near(0)
        elif j <= 6:
            step, part = (j - 1) // 2, (j - 1) % 2
            arrive(got["up", step, part])
            if step < 2 or part == 0:
                push_up(step + 1, part)
            arrive(got["down", step, part])
            if step < 2 or part == 1:
                push_down(step + 1, part)
            for n in (2 * step + 1, 2 * step + 2):
                push_near(n) if part else push_other(n)
        elif j == 7:
            arrive(got["up", 3, 0])
            push_other(7)
            arrive(got["down", 3, 1])
            push_near(7)
        if 1 <= j <= 8:
            push_x(j - 1)
        if 2 <= j <= 9:
            push_far(j - 2)
        if j == 10:
            arrive(*(got["near", n] for n in range(8)))
        if j == 11:
            arrive(*(got["far", n] for n in range(8)))

    ticks = []

    def tick():
        for j in PLAN.get(len(ticks), ()):
            gather_round(j)
        ticks.append(0)

    plain = key_bias(None)
    seam = key_bias(lat == lats - 1)
    load_x.wait()
    need("east1")
    for g in range(3):
        c[48 * g : 48 * g + 48] = mm(
            r["veast1"][...], x[384 * g : 384 * g + 384]
        ).astype(BF16)
    if remote:
        pl.semaphore_wait(barrier, len(partners))
    row_in = halo(0, x.at[pl.ds(0, 144)], x.at[pl.ds(1152, 144)], (north, lon))
    col_in = halo(1, c, xe.at[pl.ds(0, 144)], (lat, west))
    end_in = halo(2, c.at[pl.ds(0, 32)], xe.at[pl.ds(144, 32)], (north, west))
    gather_round(0)
    fetch("halo1", "wo", "we", "wr")

    fine[16:20, 48:80] = jnp.zeros((4, 32, 512), BF16)

    need("own1", "wi")
    for b in range(3):
        at = slice(320 * b, 320 * b + 240)
        wx = mm(r["vown1"][0:240], x[(6 * b + 3) * 48 : (6 * b + 9) * 48])
        xw[at] = wx.astype(BF16)
        qkv1[at] = mm(norm(wx, r["g1"][...]), r["vwi"][...]).astype(BF16)
        for k in range(3):
            attend_window(qkv1, ctx1, 320 * b + k * PAD, plain, 512)
        tick()

    fetch("east2", "join", "wm", "leave", "stay", "enter")
    arrive(row_in, col_in, end_in)
    need("halo1")
    edges = []
    for b in range(4):
        part = slice(240, 320) if b < 3 else slice(0, 320)
        wx = mm(r["vown1"][part], x[(6 * b + 3) * 48 : (6 * b + 9) * 48])
        wx = wx + mm(r["vhalo1"][b, part], xe[32 * b + 16 : 32 * b + 80])
        xw[320 * b + part.start : 320 * b + 320] = wx.astype(BF16)
        edges.append(norm(wx, r["g1"][...]))
    edges = jnp.concatenate(edges, axis=0)
    for j in range(3):
        some = slice(512 * j, 512 * j + 512)
        made = mm(edges, r["vwi"][:, some]).astype(BF16)
        for b in range(3):
            qkv1[320 * b + 240 : 320 * b + 320, some] = made[80 * b : 80 * b + 80]
        qkv1[960:1280, some] = made[240:560]
    tick()
    for b in range(3):
        attend_window(qkv1, ctx1, 320 * b + 240, plain, 512)
    tick()
    for k in range(4):
        attend_window(qkv1, ctx1, 960 + k * PAD, seam, 512)
    tick()
    need("wo", "we", "wr")

    def feed(slots):
        parts = []
        for start, count in slots:
            at = slice(PAD * start, PAD * (start + count))
            first = xw[at].astype(F32) + mm(ctx1[at], r["vwo"][...])
            parts += [first[PAD * k : PAD * k + 72] for k in range(count)]
        f = jnp.concatenate(parts, axis=0).astype(BF16).astype(F32)
        fn = norm(f, r["g2"][...])
        size = f.shape[0]
        for j in range(4):
            some = slice(512 * j, 512 * j + 512)
            hid[0:size, some] = gelu(mm(fn, r["vwe"][:, some])).astype(BF16)
            tick()
        total = f + mm(hid[0:size], r["vwr"][...])
        blank = jnp.zeros((PAD - 72, 512), F32)
        at = 0
        for start, count in slots:
            for k in range(count):
                whole = jnp.concatenate([total[at : at + 72], blank], axis=0)
                fine[start + k] = whole.astype(BF16)
                at += 72
        tick()

    feed([(0, 4), (4, 1), (8, 1), (12, 1)])
    need("east2")
    west_edge = jnp.concatenate([fine[4 * b] for b in range(4)], axis=0)
    fc[...] = mm(r["veast2"][...], west_edge).astype(BF16)
    row_in = halo(
        3, fine.at[pl.ds(0, 4), pl.ds(0, 48)], fine.at[pl.ds(16, 4), pl.ds(0, 48)], (north, lon)
    )
    col_in = halo(4, fc, fe.at[pl.ds(0, 144)], (lat, west))
    end_in = halo(5, fc.at[pl.ds(0, 32)], fe.at[pl.ds(144, 32)], (north, west))
    feed([(5, 3), (9, 3), (13, 3)])

    need("join", "wm")
    arrive(row_in, col_in, end_in)
    blocks = []
    for a in range(2):
        bands = fine[8 * a : 8 * a + 12].reshape(960, 512)
        start = (16, 80)[a]
        blocks.append(
            mm(r["vjoin"][a, :, 0:960], bands)
            + mm(r["vjoin"][a, :, 960:1056], fe[start : start + 96])
        )
    members = [
        jnp.concatenate([blocks[a][160 * k : 160 * k + 160] for a in range(2)], axis=0)
        for k in range(4)
    ]
    tick()
    mean = sum(jnp.sum(v, -1, keepdims=True) for v in members) * (1 / 2048)
    members = [v - mean for v in members]
    factor = lax.rsqrt(
        sum(jnp.sum(v * v, -1, keepdims=True) for v in members) * (1 / 2048) + EPS
    )
    joined = jnp.concatenate(
        [
            (v * factor * r["gm"][:, 512 * k : 512 * k + 512]).astype(BF16)
            for k, v in enumerate(members)
        ],
        axis=1,
    )
    wx = mm(joined, r["vwm"][...]).astype(BF16).astype(F32)
    tick()

    need("leave", "stay", "enter")
    xn = norm(wx, r["gc"][...])
    xn2[0] = xn[:, 0:512]
    xn2[1] = xn[:, 512:1024]
    depth = w.shape[0] // 2
    near = pl.ds(pl.multiple_of(y_hi * depth, depth), depth)
    far = pl.ds(pl.multiple_of((1 - y_hi) * depth, depth), depth)
    for j in range(6):
        some = slice(512 * j, 512 * j + 512)
        acc[:, some] = mm(xn2[y_hi], w[near, some])
        tick()
    for j in range(6):
        some = slice(512 * j, 512 * j + 512)
        qkv[:, some] = (acc[:, some] + mm(xn2[1 - y_hi], w[far, some])).astype(BF16)
    for k in (1, 2, 3, 0):
        attend_window(qkv, ctx, k * PAD, seam if k >= 2 else plain, 1024)
    y = (wx + mm(ctx[...], w[:, 3072:4096])).astype(BF16)
    s[...] = mm(r["vleave"][...], y).astype(BF16)
    row_back = halo(6, s.at[pl.ds(0, 64)], z.at[pl.ds(0, 64)], (south, lon))
    col_back = halo(7, s.at[pl.ds(64, 64)], z.at[pl.ds(64, 64)], (lat, east))
    end_back = halo(8, s.at[pl.ds(128, 32)], z.at[pl.ds(128, 32)], (south, east))
    kept = mm(r["vstay"][...], y)
    arrive(row_back, col_back, end_back)
    r["out"][...] = (kept + mm(r["venter"][...], z[...])).astype(BF16)
    if remote:
        for copy in sent:
            copy.wait_send()


PLAN = {
    2: (1,), 4: (2,), 6: (3,), 9: (4,), 11: (5,), 14: (6,), 15: (7,), 16: (8,), 17: (10, 9),
    23: (11,),
}


def per_device(remote, *args):
    tokens, g1, wi, wo, g2, we, wr, gm, wm, gc, ci, co = args
    consts = [jnp.asarray(t) for t in tables()]
    operands = [
        tokens.reshape(1152, 512), g1.reshape(1, -1), wi, wo, g2.reshape(1, -1), we, wr,
        gm.reshape(1, -1), wm, gc.reshape(1, -1), ci, co, *consts,
    ]
    hbm = pl.BlockSpec(memory_space=pl.ANY)
    vmem = pl.BlockSpec(memory_space=pltpu.VMEM)
    small = (1, 4, 7, 9)
    held = [wi, wo, we, wr, wm, *consts]
    scratch = [
        pltpu.VMEM((1296, 512), BF16),
        pltpu.VMEM((176, 512), BF16),
        pltpu.VMEM((144, 512), BF16),
        pltpu.VMEM((20, PAD, 512), BF16),
        pltpu.VMEM((176, 512), BF16),
        pltpu.VMEM((144, 512), BF16),
        pltpu.VMEM((160, 1024), BF16),
        pltpu.VMEM((160, 1024), BF16),
        pltpu.VMEM((1024, 4096), BF16),
        pltpu.VMEM((320, 3072), BF16),
        pltpu.VMEM((320, 1024), BF16),
        pltpu.VMEM((648, 2048), BF16),
        pltpu.VMEM((1280, 512), BF16),
        pltpu.VMEM((1280, 1536), BF16),
        pltpu.VMEM((1280, 512), BF16),
        pltpu.VMEM((2, 320, 512), BF16),
        pltpu.VMEM((320, 3072), F32),
        *(pltpu.VMEM(a.shape, BF16) for a in held),
        pltpu.SemaphoreType.DMA((3 + len(ORDER),)),
        pltpu.SemaphoreType.DMA((10,)),
        pltpu.SemaphoreType.DMA((10,)),
        pltpu.SemaphoreType.DMA((54,)),
        pltpu.SemaphoreType.DMA((54,)),
    ]
    params = dict(collective_id=0, has_side_effects=True) if remote else {}
    out = pl.pallas_call(
        functools.partial(kernel, remote),
        out_shape=jax.ShapeDtypeStruct((288, 1024), BF16),
        in_specs=[vmem if i in small else hbm for i in range(len(operands))],
        out_specs=vmem,
        scratch_shapes=scratch,
        compiler_params=pltpu.CompilerParams(vmem_limit_bytes=60 * 1024 * 1024, **params),
        name="encoder",
    )(*operands)
    return out.reshape(12, 24, 1024)


def solution(mesh, remote=True):
    return jax.shard_map(
        functools.partial(per_device, remote),
        mesh=mesh,
        in_specs=(P("lat", "lon", None), *[P()] * 9, P("lon", None), P("lon", None)),
        out_specs=P("lat", "lon", None),
        check_vma=False,
    )
```

profile of v0, /device:TPU:2, one launch (start us, length us, event | category | flops | bytes accessed | tf_op | source)
XLA Modules:
  0.0 64.7 jit_solution(14545599719450333379)
XLA Ops:
  0.0 62.7 %encoder.1 = bf16[288,1024]{1,0:T(8,128)(2,1)} custom-call(bf16[1152,512]{1,0:T(8,128)(2,1)} %bitcast.7, f32[1,512]{1,0:T(1,128)} %bitcast.10, bf16[512,1536]{1,0:T(8,128)(2,1)} %refs_2_.1, bf16[512,512]{1,0:T(8,128)(2,1)} %refs_3_.1, f32[1,512]{1,0:T(1,128)} %bitcast.11, bf16[512,2048]{1,0:T(8,128)(2,1)} %refs_5_.1, bf16[2048,512]{1,0:T(8,128)(2,1)} %refs_6_.1, ...), custom_call_target="tpu_custom_call" | custom-call | tf_op jit(solution)/shard_map/encoder/pallas_call | solution.py:507
  62.7 1.9 %copy.22 = bf16[12,24,1024]{2,1,0:T(8,128)(2,1)} copy(bf16[12,24,1024]{2,1,0:T(8,128)(2,1)} %bitcast.6) | data formatting | bytes 1179648
where the time goes:
time: 64.8 us; the launch traced here: 64.7 us
  Pallas kernels  62.7 us (97%)
  local copies, waits for them, and re-layouts  1.92 us (3%)
    pallas_call x1, Pallas kernels, per_device(): pl.pallas_call(functools.partial(kernel, remote), out_shape=jax.ShapeDtyp...  62.7 us
    unnamed x1, local copies, waits for them, and re-layouts  1.92 us

commit v1 on v0

--- a/solution.py
+++ b/solution.py
@@ -90,11 +90,11 @@
     join = np.stack(joins)
     leave = one_hot(
         160,
-        320,
-        [((r - 9) * 18 + c, window_slot(r, c, 2)) for r in range(9, 12) for c in range(18)]
-        + [(64 + r * 6 + c - 18, window_slot(r, c, 2)) for r in range(9) for c in range(18, 24)]
+        240,
+        [((r - 9) * 18 + c, window_slot(r, c, 2) - PAD) for r in range(9, 12) for c in range(18)]
+        + [(64 + r * 6 + c - 18, window_slot(r, c, 2) - PAD) for r in range(9) for c in range(18, 24)]
         + [
-            (128 + (r - 9) * 6 + c - 18, window_slot(r, c, 2))
+            (128 + (r - 9) * 6 + c - 18, window_slot(r, c, 2) - PAD)
             for r in range(9, 12)
             for c in range(18, 24)
         ],
@@ -446,14 +446,16 @@
     for j in range(6):
         some = slice(512 * j, 512 * j + 512)
         qkv[:, some] = (acc[:, some] + mm(xn2[1 - y_hi], w[far, some])).astype(BF16)
-    for k in (1, 2, 3, 0):
+    for k in (3, 2, 1):
         attend_window(qkv, ctx, k * PAD, seam if k >= 2 else plain, 1024)
-    y = (wx + mm(ctx[...], w[:, 3072:4096])).astype(BF16)
-    s[...] = mm(r["vleave"][...], y).astype(BF16)
+    y_edge = (wx[PAD:] + mm(ctx[PAD:320], w[:, 3072:4096])).astype(BF16)
+    s[...] = mm(r["vleave"][...], y_edge).astype(BF16)
     row_back = halo(6, s.at[pl.ds(0, 64)], z.at[pl.ds(0, 64)], (south, lon))
     col_back = halo(7, s.at[pl.ds(64, 64)], z.at[pl.ds(64, 64)], (lat, east))
     end_back = halo(8, s.at[pl.ds(128, 32)], z.at[pl.ds(128, 32)], (south, east))
-    kept = mm(r["vstay"][...], y)
+    attend_window(qkv, ctx, 0, plain, 1024)
+    y_rest = (wx[0:PAD] + mm(ctx[0:PAD], w[:, 3072:4096])).astype(BF16)
+    kept = mm(r["vstay"][...], jnp.concatenate([y_rest, y_edge], axis=0))
     arrive(row_back, col_back, end_back)
     r["out"][...] = (kept + mm(r["venter"][...], z[...])).astype(BF16)
     if remote:

time: 64.8 us -> 64.4 us (level)
  no operation moved by 1% of the time
where the time goes in v1:
time: 64.4 us; the launch traced here: 64.3 us
  Pallas kernels  62.3 us (97%)
  local copies, waits for them, and re-layouts  1.92 us (3%)
    pallas_call x1, Pallas kernels, per_device(): pl.pallas_call(functools.partial(kernel, remote), out_shape=jax.ShapeDtyp...  62.3 us
    unnamed x1, local copies, waits for them, and re-layouts  1.92 us

profile of v1, /device:TPU:2, one launch (start us, length us, event | category | flops | bytes accessed | tf_op | source)
XLA Modules:
  0.0 64.3 jit_solution(7070871003126835678)
XLA Ops:
  0.0 62.3 %encoder.1 = bf16[288,1024]{1,0:T(8,128)(2,1)} custom-call(bf16[1152,512]{1,0:T(8,128)(2,1)} %bitcast.7, f32[1,512]{1,0:T(1,128)} %bitcast.10, bf16[512,1536]{1,0:T(8,128)(2,1)} %refs_2_.1, bf16[512,512]{1,0:T(8,128)(2,1)} %refs_3_.1, f32[1,512]{1,0:T(1,128)} %bitcast.11, bf16[512,2048]{1,0:T(8,128)(2,1)} %refs_5_.1, bf16[2048,512]{1,0:T(8,128)(2,1)} %refs_6_.1, ...), custom_call_target="tpu_custom_call" | custom-call | tf_op jit(solution)/shard_map/encoder/pallas_call | solution.py:509
  62.3 1.9 %copy.22 = bf16[12,24,1024]{2,1,0:T(8,128)(2,1)} copy(bf16[12,24,1024]{2,1,0:T(8,128)(2,1)} %bitcast.6) | data formatting | bytes 1179648

commit v2 on v1

--- a/solution.py
+++ b/solution.py
@@ -464,7 +464,7 @@
 
 
 PLAN = {
-    2: (1,), 4: (2,), 6: (3,), 9: (4,), 11: (5,), 14: (6,), 15: (7,), 16: (8,), 17: (10, 9),
+    2: (1,), 4: (2,), 6: (3,), 9: (4,), 11: (5,), 14: (6,), 15: (7,), 17: (8, 10), 20: (9,),
     23: (11,),
 }
 

time: 64.4 us -> 65.4 us (1.016)
  Pallas kernels: 62.3 us -> 63.4 us
    pallas_call x1, Pallas kernels: 62.3 us -> 63.4 us  [per_device(): pl.pallas_call(functools.partial(kernel, remote), out_shape=jax.ShapeDtyp...]
where the time goes in v2:
time: 65.4 us; the launch traced here: 65.3 us
  Pallas kernels  63.4 us (97%)
  local copies, waits for them, and re-layouts  1.92 us (3%)
    pallas_call x1, Pallas kernels, per_device(): pl.pallas_call(functools.partial(kernel, remote), out_shape=jax.ShapeDtyp...  63.4 us
    unnamed x1, local copies, waits for them, and re-layouts  1.92 us

profile of v2, /device:TPU:2, one launch (start us, length us, event | category | flops | bytes accessed | tf_op | source)
XLA Modules:
  0.0 65.3 jit_solution(15419803404603354752)
XLA Ops:
  0.0 63.4 %encoder.1 = bf16[288,1024]{1,0:T(8,128)(2,1)} custom-call(bf16[1152,512]{1,0:T(8,128)(2,1)} %bitcast.7, f32[1,512]{1,0:T(1,128)} %bitcast.10, bf16[512,1536]{1,0:T(8,128)(2,1)} %refs_2_.1, bf16[512,512]{1,0:T(8,128)(2,1)} %refs_3_.1, f32[1,512]{1,0:T(1,128)} %bitcast.11, bf16[512,2048]{1,0:T(8,128)(2,1)} %refs_5_.1, bf16[2048,512]{1,0:T(8,128)(2,1)} %refs_6_.1, ...), custom_call_target="tpu_custom_call" | custom-call | tf_op jit(solution)/shard_map/encoder/pallas_call | solution.py:509
  63.4 1.9 %copy.22 = bf16[12,24,1024]{2,1,0:T(8,128)(2,1)} copy(bf16[12,24,1024]{2,1,0:T(8,128)(2,1)} %bitcast.6) | data formatting | bytes 1179648
